TPU v7x, 32 devices: a whole 2x2x4 slice. The times are simulated.
32 devices in a mesh: grp: 2 (over core), aux: 4 (over y, x), orb: 4 (over z).
Axes of the slice: x: 2, y: 2, z: 4, core: 2. Of those that a mesh axis runs over, the one named last changes fastest.
Arguments:
- fitted_tensor: bfloat16 [4, 8192, 8192], P('grp', 'aux', 'orb'), may hold values from -0.23925781 to 0.23925781
- block_mask: int32 [2, 64, 64], P('grp'), may hold values 0 or 1
- orbitals: bfloat16 [8192, 256], P('aux'), may hold values from -0.0625 to 0.0625
- nuclear: float32 [8192], replicated, may hold values from 0.5 to 1.5
- centres: float32 [3, 8192], replicated, may hold values from 0 to 8
- mm_positions: float32 [3, 32768], P(None, ('grp', 'aux', 'orb')), may hold values from 0 to 8
- mm_charges: float32 [32768], P(('grp', 'aux', 'orb')), may hold values from -0.12 to 0.12
- neighbours: int32 [32, 2], P(('grp', 'aux', 'orb')), may hold values from 0 to 63, all different within a row
Outputs:
- fock: float32 [8192, 8192], P(('aux', 'orb'))
- mm_potential: float32 [32768], P(('grp', 'aux', 'orb'))
Inputs may be any that keep to these rules, and one draw needn't show every extreme that they name: `neighbours`: each row names 2 different blocks; every block is named by some row.
All inputs are finite; a program needn't handle non-finite values. No bound on the sum of `block_mask` on one device may be relied on, other than what follows from the above.
Results may differ from a plain program's by a relative error of at most 0.01.
Values may be sent and summed in bfloat16 or wider, within the bound.
A program may use at most 128 MiB of HBM per device.

v0:
```python
import jax
import jax.numpy as jnp
from jax import lax
from jax.sharding import PartitionSpec as P

BLK = 128
softening = 1.0


def near_kernel(picker, centre_blocks, charge_blocks, atom_xyz):
    near_xyz = jnp.einsum("kb,cbj->ckj", picker, centre_blocks, precision=lax.Precision.HIGHEST)
    near_xyz = near_xyz.reshape(3, picker.shape[0] * centre_blocks.shape[2])
    near_q = jnp.dot(picker, charge_blocks, precision=lax.Precision.HIGHEST).reshape(-1)
    offsets = near_xyz[:, :, None] - atom_xyz[:, None, :]
    kernel = lax.rsqrt(jnp.sum(offsets * offsets, axis=0) + softening)
    return (kernel, near_q)


def add_diagonal(fock_rows, first_row, field_vec):
    row_count = fock_rows.shape[0]
    values = lax.dynamic_slice_in_dim(field_vec, first_row, row_count, 0)
    row_ids = jnp.arange(row_count, dtype=jnp.int32)[:, None]
    col_ids = jnp.arange(fock_rows.shape[1], dtype=jnp.int32)[None, :]
    on_diagonal = col_ids == first_row + row_ids
    return fock_rows + jnp.where(on_diagonal, values[:, None], jnp.float32(0.0))


def block_picker(first, count, block_total):
    positions = (first + jnp.arange(count, dtype=jnp.int32)) // BLK
    block_ids = jnp.arange(block_total, dtype=jnp.int32)
    return (positions[:, None] == block_ids[None, :]).astype(jnp.float32)


def per_device(
    fitted_tensor, block_mask, orbitals, nuclear, centres, mm_positions, mm_charges, neighbours
):
    row_span = fitted_tensor.shape[1]
    col_span = fitted_tensor.shape[2]
    orb_count = lax.axis_size("orb")
    aux_id = lax.axis_index("aux")
    orb_id = lax.axis_index("orb")
    own_span = row_span // orb_count
    block_total = block_mask.shape[1]
    whole_c = lax.all_gather(orbitals, "aux", axis=0, tiled=True)
    row_start = aux_id * row_span
    col_start = orb_id * col_span
    window_c = lax.dynamic_slice_in_dim(whole_c, col_start, col_span, 0)
    row_pick = block_picker(row_start, row_span, block_total)
    col_pick = block_picker(col_start, col_span, block_total)
    row_bits = jnp.dot(row_pick, block_mask[0].astype(jnp.float32), precision=lax.Precision.HIGHEST)
    mask_wide = jnp.dot(row_bits, col_pick.T, precision=lax.Precision.HIGHEST).astype(jnp.bfloat16)
    masked = fitted_tensor * mask_wide[None]
    x_partial = jnp.einsum("pmn,ni->pmi", masked, window_c, preferred_element_type=jnp.float32)
    x_rows = lax.psum(x_partial, "orb")
    own_rows = lax.dynamic_slice_in_dim(x_rows, orb_id * own_span, own_span, 1)
    x_own = own_rows.astype(jnp.bfloat16)
    own_c = lax.dynamic_slice_in_dim(orbitals, orb_id * own_span, own_span, 0)
    dens_part = 2.0 * jnp.einsum("pmi,mi->p", x_own, own_c, preferred_element_type=jnp.float32)
    densities = lax.psum(dens_part, ("aux", "orb")).astype(jnp.bfloat16)
    coulomb_block = jnp.einsum("pmn,p->mn", masked, densities, preferred_element_type=jnp.float32)
    coulomb = lax.all_to_all(coulomb_block, "orb", split_axis=0, concat_axis=1, tiled=True)
    c_float = whole_c.astype(jnp.float32)
    population = 2.0 * jnp.sum(c_float * c_float, axis=1)
    qm_charge = nuclear - population
    centre_blocks = centres.reshape(3, block_total, BLK)
    charge_blocks = qm_charge.reshape(block_total, BLK)
    picker = (neighbours[0][:, None] == jnp.arange(block_total, dtype=jnp.int32)[None, :]).astype(
        jnp.float32
    )
    kernel, near_q = near_kernel(picker, centre_blocks, charge_blocks, mm_positions)
    mm_potential = jnp.dot(near_q, kernel, precision=lax.Precision.HIGHEST)
    contrib = jnp.dot(kernel, mm_charges, precision=lax.Precision.HIGHEST).reshape(
        picker.shape[0], BLK
    )
    field_part = jnp.dot(picker.T, contrib, precision=lax.Precision.HIGHEST)
    field_sum = lax.psum(field_part, ("grp", "aux", "orb"))
    field_vec = field_sum.reshape(-1)
    own_first = row_start + orb_id * own_span
    exchange_part = jnp.einsum(
        "pmi,pni->mn",
        x_own,
        lax.all_gather(x_own, ("aux", "orb"), axis=1, tiled=True),
        preferred_element_type=jnp.float32,
    )
    fock_part = coulomb - 0.5 * exchange_part
    fock_sum = lax.psum(fock_part, "grp")
    fock = add_diagonal(fock_sum, own_first, field_vec)
    return (fock, mm_potential)


def solution(mesh):
    in_specs = (
        P("grp", "aux", "orb"),
        P("grp", None, None),
        P("aux", None),
        P(),
        P(),
        P(None, ("grp", "aux", "orb")),
        P(("grp", "aux", "orb")),
        P(("grp", "aux", "orb"), None),
    )
    out_specs = (P(("aux", "orb"), None), P(("grp", "aux", "orb")))
    return jax.shard_map(
        per_device, mesh=mesh, in_specs=in_specs, out_specs=out_specs, check_vma=False
    )
```

profile of v0, /device:TPU:0, one launch (start us, length us, event | category | flops | bytes accessed | tf_op | source)
XLA Modules:
  0.0 848.3 jit_solution(9946186388667584154)
XLA Ops:
  7.2 0.7 all-gather.3.cloned.1.call-update
  8.0 1.0 bitcast_convert_fusion
  9.0 1.7 fusion.6
  10.6 7.5 convolution_convert_fusion
  18.1 14.8 %broadcast_multiply_fusion = bf16[2,2048,2048]{2,1,0:T(8,128)(2,1)} fusion(bf16[2,2048,2048]{2,1,0:T(8,128)(2,1)} %param.8, bf16[2048,2048]{1,0:T(8,128)(2,1)S(1)} %convolution_convert_fusion), kind=kLoop, calls=%fused_computation.7 | loop fusion | flops 8388608 | bytes 41943040 | tf_op jit(solution)/shard_map/mul | solution.py:52
  32.9 32.4 %all-gather.3.cloned.1.call-done = bf16[8192,256]{1,0:T(8,128)(2,1)} async-done(((bf16[2048,256]{1,0:T(8,128)(2,1)}), bf16[8192,256]{1,0:T(8,128)(2,1)}) %all-gather.3.cloned.1.call-update) | async-done | bytes 4194320 | tf_op jit(solution)/shard_map/all_gather | solution.py:44
  65.3 12.5 %fusion.3 = f32[2,2048,256]{2,1,0:T(8,128)} fusion(bf16[2,2048,2048]{2,1,0:T(8,128)(2,1)} %broadcast_multiply_fusion, bf16[8192,256]{1,0:T(8,128)(2,1)} %all-gather.3.cloned.1.call-done, s32[]{:T(128)S(6)} %select_n.32), kind=kOutput, calls=%fused_computation.12 | convolution fusion | flops 4294967296 | bytes 22020100 | tf_op jit(solution)/shard_map/pmn,ni->pmi/dot_general | solution.py:53
  77.8 147.1 %all-reduce.4 = bf16[2,2048,256]{2,1,0:T(8,128)(2,1)S(1)} all-reduce(f32[2,2048,256]{2,1,0:T(8,128)} %fusion.3), channel_id=1, replica_groups=mesh['grp'=2,'aux'=4,'orb'=4] {'orb'}, use_global_device_ids=true, to_apply=%region_0.1 | all-reduce | flops 1048576 | bytes 6291456 | tf_op jit(solution)/shard_map/psum | solution.py:54
  224.9 1.0 multiply_reduce_fusion.2
  225.9 38.2 %psum.29 = bf16[2]{0:T(256)(128)(2,1)S(1)} all-reduce(f32[2]{0:T(128)S(1)} %broadcast_multiply_fusion.1), channel_id=1, replica_groups=mesh['grp'=2,'aux'=4,'orb'=4] {'aux','orb'}, use_global_device_ids=true, to_apply=%region_1.2 | all-reduce | flops 2 | bytes 12 | tf_op jit(solution)/shard_map/psum | solution.py:59
  264.2 28.8 %fusion.1 = f32[1,2048,2048]{2,0,1:T(1,128)S(1)} fusion(bf16[2,2048,2048]{2,1,0:T(8,128)(2,1)} %broadcast_multiply_fusion, bf16[2]{0:T(256)(128)(2,1)S(1)} %psum.29), kind=kOutput, calls=%fused_computation.4 | convolution fusion | flops 16777216 | bytes 33554436 | tf_op jit(solution)/shard_map/pmn,p->mn/dot_general | solution.py:60
  292.9 11.3 %copy.18 = f32[1,2048,2048]{2,1,0:T(8,128)} copy(f32[1,2048,2048]{2,0,1:T(1,128)S(1)} %fusion.1) | data formatting | bytes 33554432 | tf_op jit(solution)/shard_map/pmn,p->mn/dot_general | solution.py:60
  304.2 7.0 all-to-all-start
  311.2 0.7 all-gather.5.cloned.1.call-update
  312.0 433.2 %all-to-all-done = f32[4,512,2048]{2,1,0:T(8,128)} async-done(((f32[4,512,2048]{2,1,0:T(8,128)}), f32[4,512,2048]{2,1,0:T(8,128)}, u32[]{:S(2)}, u32[]{:S(2)}) %all-to-all-start) | async-done | bytes 16777248 | tf_op jit(solution)/shard_map/all_to_all | solution.py:61
  745.2 11.9 %copy.21 = f32[4,64,8,2048]{3,2,0,1:T(8,128)} copy(f32[4,64,8,2048]{3,2,1,0:T(8,128)} %bitcast.23) | data formatting | bytes 33554432 | tf_op jit(solution)/shard_map/all_to_all | solution.py:61
  757.0 14.4 %fusion = f32[512,8192]{1,0:T(8,128)} fusion(f32[512,8192]{1,0:T(8,128)} %bitcast.59, bf16[2,512,256]{2,1,0:T(8,128)(2,1)S(1)} %copy-done.1, bf16[2,8192,256]{2,1,0:T(8,128)(2,1)} %all-gather.5.cloned.1.call-done), kind=kOutput, calls=%fused_computation.1 | convolution fusion | flops 4303355904 | bytes 42467328 | tf_op jit(solution)/shard_map/pmi,pni->mn/dot_general | solution.py:79
  771.5 0.9 copy-done.2
  772.9 1.0 fusion.8
  774.2 37.3 %psum.31 = f32[8192]{0:T(1024)S(1)} all-reduce(f32[8192]{0:T(1024)S(1)} %convolution_bitcast_fusion), channel_id=1, replica_groups=mesh['grp'=2,'aux'=4,'orb'=4] {'grp','aux','orb'}, use_global_device_ids=true, to_apply=%region_4.5 | all-reduce | flops 8192 | bytes 65536 | tf_op jit(solution)/shard_map/psum | solution.py:76
  811.6 3.8 multiply_reduce_fusion
  815.5 1.3 fusion.7
  816.8 12.9 %all-reduce.3.cloned.1.call-done = f32[512,8192]{1,0:T(8,128)} async-done(((f32[512,8192]{1,0:T(8,128)}), f32[512,8192]{1,0:T(8,128)}) %all-reduce.3.cloned.1.call-update) | async-done | bytes 16777232 | tf_op jit(solution)/shard_map/psum | solution.py:86
  829.7 12.1 %select_add_fusion = f32[512,8192]{1,0:T(8,128)} fusion(f32[512,8192]{1,0:T(8,128)} %all-reduce.3.cloned.1.call-done, f32[512]{0:T(512)S(1)} %dynamic_slice.15, s32[512]{0:T(512)S(1)} %iota_add_fusion.2), kind=kLoop, calls=%fused_computation.2 | loop fusion | flops 12582912 | bytes 33558528 | tf_op jit(solution)/shard_map/add | solution.py:25
  (26 shorter events, 1.3 us)
Async XLA Ops:
  7.2 765.8 %copy-start = (f32[1024]{0:T(1024)S(1)}, f32[1024]{0:T(1024)}, u32[]{:S(2)}) copy-start(f32[1024]{0:T(1024)} %param.14) | copy-start | bytes 12292
  7.2 58.1 %all-gather.3.cloned.1.call-start = ((), (), s32[]{:S(2)}) async-start(), calls=%async_computation.1 | async-start | bytes 5242880 | tf_op jit(solution)/shard_map/all_gather | solution.py:44
  304.2 440.9 %all-to-all-start = ((f32[4,512,2048]{2,1,0:T(8,128)}), f32[4,512,2048]{2,1,0:T(8,128)}, u32[]{:S(2)}, u32[]{:S(2)}) async-start(f32[4,512,2048]{2,1,0:T(8,128)} %bitcast.58), calls=%async_computation | async-start | bytes 33554432 | tf_op jit(solution)/shard_map/all_to_all | solution.py:61
  311.2 445.8 %all-gather.5.cloned.1.call-start = ((), (), s32[]{:S(2)}) async-start(), calls=%async_computation.2 | async-start | bytes 8912896 | tf_op jit(solution)/shard_map/all_gather | solution.py:82
  312.0 517.8 %all-reduce.3.cloned.1.call-start = ((), (), s32[]{:S(2)}) async-start(), calls=%async_computation.3 | async-start | bytes 33554432 | tf_op jit(solution)/shard_map/psum | solution.py:86
  745.2 11.9 %copy-start.1 = (bf16[2,512,256]{2,1,0:T(8,128)(2,1)S(1)}, bf16[2,512,256]{2,1,0:T(8,128)(2,1)}, u32[]{:S(2)}) copy-start(bf16[2,512,256]{2,1,0:T(8,128)(2,1)} %get-tuple-element.3) | copy-start | bytes 1572868
  771.4 0.9 copy-start.2
  771.4 0.9 copy-start.5
  771.4 1.1 copy-start.4
  771.4 43.9 %copy-start.3 = (f32[8192]{0:T(1024)S(1)}, f32[8192]{0:T(1024)}, u32[]{:S(2)}) copy-start(f32[8192]{0:T(1024)} %param.11) | copy-start | bytes 98308
Sparse Core Ops, SparseCore 0:
  9.9 55.3 all-gather.2
  314.8 381.6 all-gather.4
  771.6 58.0 all-reduce.2
where the time goes:
time: 849 us; the launch traced here: 848 us
  waiting for transfers between devices  480 us (57%)
  blocking collectives  223 us (26%)
  matrix products  67.7 us (8%)
  other arithmetic  33.1 us (4%)
  local copies, waits for them, and re-layouts  24.2 us (3%)
  between operations  13.9 us (2%)
    all_to_all x1, waiting for transfers between devices, per_device(): lax.all_to_all(coulomb_block, 'orb', split_axis=0, concat_axis=1, tiled=T...  433 us
    psum x1, blocking collectives, per_device(): x_rows = lax.psum(x_partial, 'orb')  147 us
    psum x1, blocking collectives, per_device(): densities = lax.psum(dens_part, ('aux', 'orb')).astype(jnp.bfloat16)  38.2 us
    psum x1, blocking collectives, per_device(): field_sum = lax.psum(field_part, ('grp', 'aux', 'orb'))  37.3 us
    all_gather x1, waiting for transfers between devices, per_device(): whole_c = lax.all_gather(orbitals, 'aux', axis=0, tiled=True)  32.4 us
    dot_general x1, matrix products, per_device(): jnp.einsum('pmn,p->mn', masked, densities, preferred_element_type=jnp.flo...  28.8 us
  transfers between devices with their start and end apart: 4, of which 3 were waited for; matrix products, arithmetic and copies ran while one was open for 5% of the time, Pallas kernels for 0%

commit v1 on v0

--- a/solution.py
+++ b/solution.py
@@ -5,6 +5,10 @@
 
 BLK = 128
 softening = 1.0
+
+
+def guide_axis_part(piece_in):
+    return lax.psum(lax.psum(piece_in, ("aux", "orb")), "grp")
 
 
 def near_kernel(picker, centre_blocks, charge_blocks, atom_xyz):
@@ -73,7 +77,7 @@
         picker.shape[0], BLK
     )
     field_part = jnp.dot(picker.T, contrib, precision=lax.Precision.HIGHEST)
-    field_sum = lax.psum(field_part, ("grp", "aux", "orb"))
+    field_sum = guide_axis_part(field_part)
     field_vec = field_sum.reshape(-1)
     own_first = row_start + orb_id * own_span
     exchange_part = jnp.einsum(

time: 849 us -> 878 us (1.034)
  waiting for transfers between devices: 480 us -> 505 us
    psum x1, waiting for transfers between devices: 12.9 us -> 49.1 us  [per_device(): fock_sum = lax.psum(fock_part, 'grp')]
    psum x1, blocking collectives: 38.2 us -> 73.3 us  [per_device(): densities = lax.psum(dens_part, ('aux', 'orb')).astype(jnp.bfloat16)]
    psum x1, blocking collectives: 37.3 us -> 3.41 us  [guide_axis_part(): return lax.psum(lax.psum(piece_in, ('aux', 'orb')), 'grp')]
where the time goes in v1:
time: 878 us
  waiting for transfers between devices  505 us (58%)
  blocking collectives  224 us (26%)
  matrix products  69.3 us (8%)
  other arithmetic  34.7 us (4%)
  local copies, waits for them, and re-layouts  23.3 us (3%)
  between operations  13.9 us (2%)
    all_to_all x1, waiting for transfers between devices, per_device(): lax.all_to_all(coulomb_block, 'orb', split_axis=0, concat_axis=1, tiled=T...  426 us
    psum x1, blocking collectives, per_device(): x_rows = lax.psum(x_partial, 'orb')  147 us
    psum x1, blocking collectives, per_device(): densities = lax.psum(dens_part, ('aux', 'orb')).astype(jnp.bfloat16)  73.3 us
    psum x1, waiting for transfers between devices, per_device(): fock_sum = lax.psum(fock_part, 'grp')  49.1 us
    dot_general x1, matrix products, per_device(): jnp.einsum('pmn,p->mn', masked, densities, preferred_element_type=jnp.flo...  28.8 us
    all_gather x1, waiting for transfers between devices, per_device(): whole_c = lax.all_gather(orbitals, 'aux', axis=0, tiled=True)  28.5 us
  transfers between devices with their start and end apart: 4, of which 3 were waited for; matrix products, arithmetic and copies ran while one was open for 5% of the time, Pallas kernels for 0%

profile of v1, /device:TPU:0, one launch (start us, length us, event | category | flops | bytes accessed | tf_op | source)
XLA Modules:
  0.0 877.6 jit_solution(1306730533184363830)
XLA Ops:
  7.9 1.1 convolution_bitcast_fusion
  9.1 1.0 bitcast_convert_fusion
  10.1 1.2 multiply_reduce_fusion.1
  11.3 1.0 fusion.8
  12.2 1.0 fusion.29
  13.2 1.7 fusion.6
  14.9 7.5 convolution_convert_fusion
  22.4 14.4 %broadcast_multiply_fusion = bf16[2,2048,2048]{2,1,0:T(8,128)(2,1)} fusion(bf16[2,2048,2048]{2,1,0:T(8,128)(2,1)} %param.8, bf16[2048,2048]{1,0:T(8,128)(2,1)S(1)} %convolution_convert_fusion), kind=kLoop, calls=%fused_computation.7 | loop fusion | flops 8388608 | bytes 41943040 | tf_op jit(solution)/shard_map/mul | solution.py:56
  36.8 28.5 %all-gather.3.cloned.1.call-done = bf16[8192,256]{1,0:T(8,128)(2,1)} async-done(((bf16[2048,256]{1,0:T(8,128)(2,1)}), bf16[8192,256]{1,0:T(8,128)(2,1)}) %all-gather.3.cloned.1.call-update) | async-done | bytes 4194320 | tf_op jit(solution)/shard_map/all_gather | solution.py:48
  65.3 12.5 %fusion.3 = f32[2,2048,256]{2,1,0:T(8,128)} fusion(bf16[2,2048,2048]{2,1,0:T(8,128)(2,1)} %broadcast_multiply_fusion, bf16[8192,256]{1,0:T(8,128)(2,1)} %all-gather.3.cloned.1.call-done, s32[]{:T(128)S(6)} %select_n.32), kind=kOutput, calls=%fused_computation.11 | convolution fusion | flops 4294967296 | bytes 22020100 | tf_op jit(solution)/shard_map/pmn,ni->pmi/dot_general | solution.py:57
  77.8 147.4 %all-reduce.5 = bf16[2,2048,256]{2,1,0:T(8,128)(2,1)} all-reduce(f32[2,2048,256]{2,1,0:T(8,128)} %fusion.3), channel_id=1, replica_groups=mesh['grp'=2,'aux'=4,'orb'=4] {'orb'}, use_global_device_ids=true, to_apply=%region_0.1 | all-reduce | flops 1048576 | bytes 6291456 | tf_op jit(solution)/shard_map/psum | solution.py:58
  225.2 2.1 multiply_reduce_fusion.2
  227.3 73.3 %all-reduce = (bf16[2]{0:T(256)(128)(2,1)S(1)}, f32[64,128]{1,0:T(8,128)S(1)}) all-reduce(f32[2]{0:T(128)S(1)} %broadcast_multiply_fusion.1, f32[64,128]{1,0:T(8,128)S(1)} %fusion.29), channel_id=1, replica_groups=mesh['grp'=2,'aux'=4,'orb'=4] {'aux','orb'}, use_global_device_ids=true, to_apply=%region_1.2 | all-reduce | flops 8194 | bytes 65548 | tf_op jit(solution)/shard_map/psum | solution.py:63
  300.6 28.8 %fusion.1 = f32[1,2048,2048]{2,0,1:T(1,128)S(1)} fusion(bf16[2,2048,2048]{2,1,0:T(8,128)(2,1)} %broadcast_multiply_fusion, bf16[2]{0:T(256)(128)(2,1)S(1)} %get-tuple-element.2), kind=kOutput, calls=%fused_computation.4 | convolution fusion | flops 16777216 | bytes 33554436 | tf_op jit(solution)/shard_map/pmn,p->mn/dot_general | solution.py:64
  329.3 11.3 %copy.18 = f32[1,2048,2048]{2,1,0:T(8,128)} copy(f32[1,2048,2048]{2,0,1:T(1,128)S(1)} %fusion.1) | data formatting | bytes 33554432 | tf_op jit(solution)/shard_map/pmn,p->mn/dot_general | solution.py:64
  340.7 7.0 all-to-all-start
  348.4 426.2 %all-to-all-done = f32[4,512,2048]{2,1,0:T(8,128)} async-done(((f32[4,512,2048]{2,1,0:T(8,128)}), f32[4,512,2048]{2,1,0:T(8,128)}, u32[]{:S(2)}, u32[]{:S(2)}) %all-to-all-start) | async-done | bytes 16777248 | tf_op jit(solution)/shard_map/all_to_all | solution.py:65
  774.6 11.9 %copy.21 = f32[4,64,8,2048]{3,2,0,1:T(8,128)} copy(f32[4,64,8,2048]{3,2,1,0:T(8,128)} %bitcast.23) | data formatting | bytes 33554432 | tf_op jit(solution)/shard_map/all_to_all | solution.py:65
  786.5 14.4 %fusion = f32[512,8192]{1,0:T(8,128)} fusion(f32[512,8192]{1,0:T(8,128)} %bitcast.58, bf16[2,512,256]{2,1,0:T(8,128)(2,1)S(1)} %copy-done.2, bf16[2,8192,256]{2,1,0:T(8,128)(2,1)} %all-gather.5.cloned.1.call-done), kind=kOutput, calls=%fused_computation.1 | convolution fusion | flops 4303355904 | bytes 42467328 | tf_op jit(solution)/shard_map/pmi,pni->mn/dot_general | solution.py:83
  800.9 3.4 psum.39
  804.4 3.9 multiply_reduce_fusion
  808.6 1.3 fusion.7
  809.8 49.1 %all-reduce.4.cloned.1.call-done = f32[512,8192]{1,0:T(8,128)} async-done(((f32[512,8192]{1,0:T(8,128)}), f32[512,8192]{1,0:T(8,128)}) %all-reduce.4.cloned.1.call-update) | async-done | bytes 16777232 | tf_op jit(solution)/shard_map/psum | solution.py:90
  859.0 12.1 %select_add_fusion = f32[512,8192]{1,0:T(8,128)} fusion(f32[512,8192]{1,0:T(8,128)} %all-reduce.4.cloned.1.call-done, f32[512]{0:T(512)S(1)} %dynamic_slice.15, s32[512]{0:T(512)S(1)} %iota_add_fusion.2), kind=kLoop, calls=%fused_computation.2 | loop fusion | flops 12582912 | bytes 33558528 | tf_op jit(solution)/shard_map/add | solution.py:29
  (24 shorter events, 1.8 us)
Async XLA Ops:
  7.2 4.1 copy-start
  7.2 58.1 %all-gather.3.cloned.1.call-start = ((), (), s32[]{:S(2)}) async-start(), calls=%async_computation.1 | async-start | bytes 5242880 | tf_op jit(solution)/shard_map/all_gather | solution.py:48
  340.7 434.0 %all-to-all-start = ((f32[4,512,2048]{2,1,0:T(8,128)}), f32[4,512,2048]{2,1,0:T(8,128)}, u32[]{:S(2)}, u32[]{:S(2)}) async-start(f32[4,512,2048]{2,1,0:T(8,128)} %bitcast.57), calls=%async_computation | async-start | bytes 33554432 | tf_op jit(solution)/shard_map/all_to_all | solution.py:65
  347.6 438.9 %all-gather.5.cloned.1.call-start = ((), (), s32[]{:S(2)}) async-start(), calls=%async_computation.2 | async-start | bytes 8912896 | tf_op jit(solution)/shard_map/all_gather | solution.py:86
  348.4 510.6 %all-reduce.4.cloned.1.call-start = ((), (), s32[]{:S(2)}) async-start(), calls=%async_computation.3 | async-start | bytes 33554432 | tf_op jit(solution)/shard_map/psum | solution.py:90
  774.6 11.9 %copy-start.2 = (bf16[2,512,256]{2,1,0:T(8,128)(2,1)S(1)}, bf16[2,512,256]{2,1,0:T(8,128)(2,1)}, u32[]{:S(2)}) copy-start(bf16[2,512,256]{2,1,0:T(8,128)(2,1)} %get-tuple-element.5) | copy-start | bytes 1572868
  800.9 7.5 copy-start.3
  800.9 7.5 copy-start.4
  808.6 62.5 %copy-start.1 = (f32[1024]{0:T(1024)S(1)}, f32[1024]{0:T(1024)}, u32[]{:S(2)}) copy-start(f32[1024]{0:T(1024)} %param.14) | copy-start | bytes 12292
Sparse Core Ops, SparseCore 0:
  9.9 55.3 all-gather.2
  351.3 367.7 all-gather.4
  801.0 57.8 all-reduce.3
